TPU v7x, 32 devices: a whole 2x2x4 slice. The times are simulated.
32 devices in a mesh: groups: 2 (over y), blk: 4 (over z), dim: 2 (over x), rep: 2 (over core).
Axes of the slice: x: 2, y: 2, z: 4, core: 2. Of those that a mesh axis runs over, the one named last changes fastest.
Arguments:
- train_grads: bfloat16 [8192, 8192], P(('groups', 'blk'), 'dim'), parts along dimension 0, may hold values from -6 to 6
- query_grads: bfloat16 [2048, 8192], P(('groups', 'rep', 'blk'), 'dim'), parts along dimension 0, may hold values from -0.0625 to 0.0625
- precond: float32 [8192], P('dim'), may hold values from 0.1 to 1
- candidates: int32 [64, 8], P(('groups', 'blk'), 'rep'), parts along dimension 0, may hold values from 0 to 1, as said below
Outputs:
- scores: float32 [8192, 1024], P(('groups', 'blk', 'dim'), 'rep'), parts along dimension 0
There are 2 independent parts, one for each index of `groups`. A program takes and returns all parts, laid end to end along the dimension named above; an argument that names none is the same for every part. Nothing has to cross between parts.
Inputs may be any that keep to these rules, and one draw needn't show every extreme that they name: `candidates`: each index of blk holds its tiles' entries with its own density, drawn from eighths of one to one.
All inputs are finite; a program needn't handle non-finite values.
Results may differ from a plain program's by a relative error of at most 0.0029.
Values may be sent and summed in bfloat16 or wider, within the bound.
A program may use at most 128 MiB of HBM per device.

v0:
```python
import jax
import jax.numpy as jnp
from jax import lax
from jax.sharding import PartitionSpec as P


def from_behind(array, axis, by):
    devices = lax.axis_size(axis)
    return lax.ppermute(array, axis, [(i, (i + by) % devices) for i in range(devices)])


def block_scores(train_grads, piece):
    return lax.dot_general(
        train_grads, piece, (((1,), (1,)), ((), ())), preferred_element_type=jnp.float32
    )


def body(train_grads, query_grads, precond, candidates):
    prepared = (query_grads.astype(jnp.float32) * lax.rsqrt(precond)[None, :]).astype(jnp.bfloat16)
    rows = train_grads.shape[0]
    width = prepared.shape[0]
    blocks = lax.axis_size("blk")
    tiles = candidates.shape[0]
    keep = candidates.astype(jnp.float32)
    position = lax.axis_index("blk")
    partial_value = jnp.zeros((rows, width * blocks), jnp.float32)

    def place(total, held, step):
        owner = (position - step) % blocks
        return lax.dynamic_update_slice(
            total, block_scores(train_grads, held), (jnp.int32(0), owner * width)
        )

    partial_value = place(partial_value, prepared, 0)

    def advance(step, state):
        total, held = state
        held = from_behind(held, "blk", 1)
        return (place(total, held, step), held)

    partial_value, unused_held = lax.fori_loop(1, blocks, advance, (partial_value, prepared))
    masked = partial_value.reshape(tiles, rows // tiles, blocks, width) * keep[:, None, :, None]
    return lax.psum_scatter(
        masked.reshape(rows, width * blocks), "dim", scatter_dimension=0, tiled=True
    )


def solution(mesh):
    in_specs = (
        P(("groups", "blk"), "dim"),
        P(("groups", "rep", "blk"), "dim"),
        P("dim"),
        P(("groups", "blk"), "rep"),
    )
    out_specs = P(("groups", "blk", "dim"), "rep")
    return jax.shard_map(body, mesh=mesh, in_specs=in_specs, out_specs=out_specs, check_vma=False)
```

profile of v0, /device:TPU:0, one launch (start us, length us, event | category | flops | bytes accessed | tf_op | source)
XLA Modules:
  0.0 155.8 jit_solution(15130649030786735511)
XLA Ops:
  6.5 0.7 rsqrt.3
  7.3 1.4 multiply_convert_fusion
  8.7 1.0 copy-done
  9.7 6.3 %convolution_bitcast_fusion = f32[1024,128]{0,1:T(8,128)S(1)} fusion(bf16[128,4096]{1,0:T(8,128)(2,1)S(1)} %multiply_convert_fusion, bf16[1024,4096]{1,0:T(8,128)(2,1)} %param.6), kind=kOutput, calls=%fused_computation.3 | convolution fusion | flops 1073741824 | bytes 9961472 | tf_op jit(solution)/shard_map/dot_general | solution.py:13
  16.0 0.2 copy.5
  16.2 0.1 copy.6
  16.3 0.2 broadcast_in_dim.2
  16.6 0.1 constant_dynamic-update-slice_fusion
  16.7 100.4 %while.17 = (s32[]{:T(128)}, f32[1024,512]{1,0:T(8,128)S(1)}, bf16[128,4096]{1,0:T(8,128)(2,1)}, bf16[1024,4096]{1,0:T(8,128)(2,1)}, s32[]{:T(128)}, /*index=5*/...) while((s32[]{:T(128)}, f32[1024,512]{1,0:T(8,128)S(1)}, ...), condition=%wide.region_1.2_spmd, body=%wide.region_0.1_spmd.sunk | while | flops 1073741824 | bytes 16253248 | solution.py:41
  16.7 3.1 %collective-permute-start = (bf16[128,4096]{1,0:T(8,128)(2,1)}, bf16[128,4096]{1,0:T(8,128)(2,1)S(1)}, u32[]{:S(2)}, u32[]{:S(2)}) collective-permute-start(bf16[128,4096]{1,0:T(8,128)(2,1)} %get-tuple-element.193), channel_id=1, source_target_pairs={{0,4},{4,8},{8,12},{12,0},{1,5},{5,9},{9,13},{13,1},{2,6},{6,10},{... | collective-permute-start | bytes 3145736 | tf_op jit(solution)/shard_map/while/body/eval_jaxpr/ppermute | solution.py:9
  19.7 25.4 %collective-permute-done = bf16[128,4096]{1,0:T(8,128)(2,1)S(1)} collective-permute-done((bf16[128,4096]{1,0:T(8,128)(2,1)}, bf16[128,4096]{1,0:T(8,128)(2,1)S(1)}, u32[]{:S(2)}, u32[]{:S(2)}) %collective-permute-start) | collective-permute-done | bytes 1048608 | tf_op jit(solution)/shard_map/while/body/eval_jaxpr/ppermute | solution.py:9
  45.1 1.0 copy.19
  46.1 5.7 %convolution_dynamic-update-slice_fusion.2 = f32[1024,512]{1,0:T(8,128)S(1)} fusion(f32[1024,512]{1,0:T(8,128)S(1)} %get-tuple-element.192, s32[]{:T(128)S(6)} %select_n.42, bf16[1024,4096]{1,0:T(8,128)(2,1)} %get-tuple-element.205, bf16[128,4096]{1,0:T(8,128)(2,1)S(1)} %collective-permute-done), kind=kOutput, calls=%fused_computation.clone.1 | convolution fusion | flops 1073741824 | bytes 9961476 | tf_op jit(solution)/shard_map/while/body/eval_jaxpr/dot_general | solution.py:13
  51.8 0.1 collective-permute-start
  51.9 26.3 %collective-permute-done = bf16[128,4096]{1,0:T(8,128)(2,1)S(1)} collective-permute-done((bf16[128,4096]{1,0:T(8,128)(2,1)}, bf16[128,4096]{1,0:T(8,128)(2,1)S(1)}, u32[]{:S(2)}, u32[]{:S(2)}) %collective-permute-start) | collective-permute-done | bytes 1048608 | tf_op jit(solution)/shard_map/while/body/eval_jaxpr/ppermute | solution.py:9
  78.2 1.0 copy.19
  79.2 5.7 %convolution_dynamic-update-slice_fusion.2 = f32[1024,512]{1,0:T(8,128)S(1)} fusion(f32[1024,512]{1,0:T(8,128)S(1)} %get-tuple-element.192, s32[]{:T(128)S(6)} %select_n.42, bf16[1024,4096]{1,0:T(8,128)(2,1)} %get-tuple-element.205, bf16[128,4096]{1,0:T(8,128)(2,1)S(1)} %collective-permute-done), kind=kOutput, calls=%fused_computation.clone.1 | convolution fusion | flops 1073741824 | bytes 9961476 | tf_op jit(solution)/shard_map/while/body/eval_jaxpr/dot_general | solution.py:13
  84.9 0.1 collective-permute-start
  85.0 25.4 %collective-permute-done = bf16[128,4096]{1,0:T(8,128)(2,1)S(1)} collective-permute-done((bf16[128,4096]{1,0:T(8,128)(2,1)}, bf16[128,4096]{1,0:T(8,128)(2,1)S(1)}, u32[]{:S(2)}, u32[]{:S(2)}) %collective-permute-start) | collective-permute-done | bytes 1048608 | tf_op jit(solution)/shard_map/while/body/eval_jaxpr/ppermute | solution.py:9
  110.4 1.0 copy.19
  111.4 5.7 %convolution_dynamic-update-slice_fusion.2 = f32[1024,512]{1,0:T(8,128)S(1)} fusion(f32[1024,512]{1,0:T(8,128)S(1)} %get-tuple-element.192, s32[]{:T(128)S(6)} %select_n.42, bf16[1024,4096]{1,0:T(8,128)(2,1)} %get-tuple-element.205, bf16[128,4096]{1,0:T(8,128)(2,1)S(1)} %collective-permute-done), kind=kOutput, calls=%fused_computation.clone.1 | convolution fusion | flops 1073741824 | bytes 9961476 | tf_op jit(solution)/shard_map/while/body/eval_jaxpr/dot_general | solution.py:13
  117.1 0.3 mul.35
  117.4 1.8 %bitcast_multiply_fusion = f32[1024,512]{1,0:T(8,128)} fusion(f32[1024,512]{1,0:T(8,128)S(1)} %get-tuple-element.138, f32[128,8,4,128]{3,2,1,0:T(4,128)S(1)} %bitcast.14), kind=kLoop, calls=%fused_computation.1 | loop fusion | flops 524288 | bytes 6291456 | tf_op jit(solution)/shard_map/mul | solution.py:42
  119.3 29.7 %reduce-scatter.2.cloned.1.call-done = f32[512,512]{1,0:T(8,128)} async-done(((f32[1024,512]{1,0:T(8,128)}), f32[512,512]{1,0:T(8,128)}) %reduce-scatter.2.cloned.1.call-update) | async-done | bytes 1048592 | tf_op jit(solution)/shard_map/reduce_scatter | solution.py:43
  (6 shorter events, 0.0 us)
Async XLA Ops:
  6.5 142.4 %reduce-scatter.2.cloned.1.call-start = ((), (), s32[]{:S(2)}) async-start(), calls=%async_computation.1 | async-start | bytes 3145728 | tf_op jit(solution)/shard_map/reduce_scatter | solution.py:43
  8.7 1.0 copy-start
  9.7 6.6 %copy-start.1 = (s32[8,4]{0,1:T(4,128)S(1)}, s32[8,4]{0,1:T(4,128)}, u32[]{:S(2)}) copy-start(s32[8,4]{0,1:T(4,128)} %param.9) | copy-start | bytes 388
  16.7 28.5 %collective-permute-start = (bf16[128,4096]{1,0:T(8,128)(2,1)}, bf16[128,4096]{1,0:T(8,128)(2,1)S(1)}, u32[]{:S(2)}, u32[]{:S(2)}) collective-permute-start(bf16[128,4096]{1,0:T(8,128)(2,1)} %get-tuple-element.193), channel_id=1, source_target_pairs={{0,4},{4,8},{8,12},{12,0},{1,5},{5,9},{9,13},{13,1},{2,6},{6,10},{... | collective-permute-start | bytes 3145736 | tf_op jit(solution)/shard_map/while/body/eval_jaxpr/ppermute | solution.py:9
  51.8 26.4 %collective-permute-start = (bf16[128,4096]{1,0:T(8,128)(2,1)}, bf16[128,4096]{1,0:T(8,128)(2,1)S(1)}, u32[]{:S(2)}, u32[]{:S(2)}) collective-permute-start(bf16[128,4096]{1,0:T(8,128)(2,1)} %get-tuple-element.193), channel_id=1, source_target_pairs={{0,4},{4,8},{8,12},{12,0},{1,5},{5,9},{9,13},{13,1},{2,6},{6,10},{... | collective-permute-start | bytes 3145736 | tf_op jit(solution)/shard_map/while/body/eval_jaxpr/ppermute | solution.py:9
  84.9 25.5 %collective-permute-start = (bf16[128,4096]{1,0:T(8,128)(2,1)}, bf16[128,4096]{1,0:T(8,128)(2,1)S(1)}, u32[]{:S(2)}, u32[]{:S(2)}) collective-permute-start(bf16[128,4096]{1,0:T(8,128)(2,1)} %get-tuple-element.193), channel_id=1, source_target_pairs={{0,4},{4,8},{8,12},{12,0},{1,5},{5,9},{9,13},{13,1},{2,6},{6,10},{... | collective-permute-start | bytes 3145736 | tf_op jit(solution)/shard_map/while/body/eval_jaxpr/ppermute | solution.py:9
Sparse Core Ops, SparseCore 0:
  119.4 29.5 reduce-scatter.1
where the time goes:
time: 156 us
  waiting for transfers between devices  107 us (69%)
  matrix products  23.5 us (15%)
  between operations  13.5 us (9%)
  local copies, waits for them, and re-layouts  5.53 us (4%)
  other arithmetic  3.23 us (2%)
  starting transfers between devices  3.2 us (2%)
    ppermute x3, waiting for transfers between devices, from_behind(): lax.ppermute(array, axis, [(i, (i + by) % devices) for i in range(devices)])  77.1 us
    reduce_scatter x1, waiting for transfers between devices, body(): lax.psum_scatter(masked.reshape(rows, width * blocks), 'dim', scatter_dim...  29.7 us
    dot_general x4, matrix products, block_scores(): lax.dot_general(train_grads, piece, (((1,), (1,)), ((), ())), preferred_e...  23.5 us
    ppermute x3, starting transfers between devices, from_behind(): lax.ppermute(array, axis, [(i, (i + by) % devices) for i in range(devices)])  3.19 us
  transfers between devices with their start and end apart: 4, of which 4 were waited for; matrix products, arithmetic and copies ran while one was open for 0% of the time, Pallas kernels for 0%

commit v1 on v0

v1 whole, which is shorter than its diff:
```python
import functools

import jax
import jax.numpy as jnp
from jax import lax
from jax.experimental import pallas as pl
from jax.experimental.pallas import tpu as pltpu
from jax.sharding import PartitionSpec as P

MESH = pl.DeviceIdType.MESH


def kernel(
    nb, nd, query, precond, keep, train_hbm, own_hbm, got_hbm,
    train, held, acc_hi, acc_lo, out_buf, part_buf,
    train_sem, send_lo, send_hi, recv, part_send, part_recv, own_sem,
):
    chunks, rows, depth = train.shape
    width = held.shape[2]
    half = rows // nd
    tiles = keep.shape[0]
    tile = rows // tiles
    z = lax.axis_index("blk")
    x = lax.axis_index("dim")
    has_lo = z > 0
    has_hi = z < nb - 1
    barrier = pltpu.get_barrier_semaphore()

    @pl.when(has_lo)
    def _():
        pl.semaphore_signal(barrier, inc=1, device_id={"blk": z - 1}, device_id_type=MESH)

    @pl.when(has_hi)
    def _():
        pl.semaphore_signal(barrier, inc=1, device_id={"blk": z + 1}, device_id_type=MESH)

    for d in range(1, nd):
        pl.semaphore_signal(
            barrier, inc=1, device_id={"dim": lax.rem(x + d, nd)}, device_id_type=MESH
        )

    def load(c):
        return pltpu.make_async_copy(
            train_hbm.at[:, pl.ds(c * depth, depth)], train.at[c], train_sem.at[c]
        )

    for c in range(chunks):
        load(c).start()

    def to_lo(b, c):
        return pltpu.make_async_remote_copy(
            src_ref=held.at[b, c], dst_ref=held.at[b, c],
            send_sem=send_lo.at[b, c], recv_sem=recv.at[b, c],
            device_id={"blk": z - 1}, device_id_type=MESH,
        )

    def to_hi(b, c):
        return pltpu.make_async_remote_copy(
            src_ref=held.at[b, c], dst_ref=held.at[b, c],
            send_sem=send_hi.at[b, c], recv_sem=recv.at[b, c],
            device_id={"blk": z + 1}, device_id_type=MESH,
        )

    def prepare(c):
        span = slice(c * depth, (c + 1) * depth)
        scale = lax.rsqrt(precond[:, span])
        held[z, c] = (query[:, span].astype(jnp.float32) * scale).astype(jnp.bfloat16)

    prepare(0)
    between = has_lo & has_hi

    @pl.when(between)
    def _():
        pl.semaphore_wait(barrier, nd + 1)

    @pl.when(jnp.logical_not(between))
    def _():
        pl.semaphore_wait(barrier, nd)

    for c in range(chunks):
        if c:
            prepare(c)

        @pl.when(has_lo)
        def _():
            to_lo(z, c).start()

        @pl.when(has_hi)
        def _():
            to_hi(z, c).start()

    def add_chunk(acc, b, c):
        block = held[b, c]

        def one(i, carry):
            at = pl.ds(pl.multiple_of(i * 256, 256), 256)
            value = lax.dot_general(
                train[c, at, :], block, (((1,), (1,)), ((), ())),
                preferred_element_type=jnp.float32,
            )

            @pl.when(c == 0)
            def _():
                acc[at, :] = value

            @pl.when(c > 0)
            def _():
                acc[at, :] += value

            return carry

        lax.fori_loop(0, rows // 256, one, 0)

    def part_copy(b, d):
        return pltpu.make_async_remote_copy(
            src_ref=part_buf.at[d - 1, b],
            dst_ref=got_hbm.at[d - 1, :, pl.ds(pl.multiple_of(b * width, width), width)],
            send_sem=part_send.at[d - 1, b], recv_sem=part_recv.at[d - 1, b],
            device_id={"dim": lax.rem(x + d, nd)}, device_id_type=MESH,
        )

    def own_copy(b):
        return pltpu.make_async_copy(
            out_buf.at[b],
            own_hbm.at[:, pl.ds(pl.multiple_of(b * width, width), width)],
            own_sem.at[b],
        )

    def masked(acc, b, first):
        values = []
        for i in range(half // tile):
            t = first * (half // tile) + i
            at = pl.ds(pl.multiple_of(t * tile, tile), tile)
            values.append(acc[at, :] * keep[t, b].astype(jnp.float32))
        return values

    def finish(acc, b):
        for d in range(1, nd):
            for i, value in enumerate(masked(acc, b, lax.rem(x + d, nd))):
                part_buf[d - 1, b, i * tile : (i + 1) * tile, :] = value.astype(jnp.bfloat16)
            part_copy(b, d).start()
        for i, value in enumerate(masked(acc, b, x)):
            out_buf[b, i * tile : (i + 1) * tile, :] = value
        own_copy(b).start()

    for c in range(chunks):
        load(c).wait()

    def own_chunk(c, carry):
        add_chunk(acc_hi, z, c)
        return carry

    lax.fori_loop(0, chunks, own_chunk, 0)
    finish(acc_hi, z)

    def step(s, carry):
        hi, lo = z + s, z - s

        def chunk(c, carry):
            @pl.when(hi < nb)
            def _():
                to_lo(hi, c).wait_recv()

                @pl.when(has_lo)
                def _():
                    to_lo(hi, c).start()

            @pl.when(lo >= 0)
            def _():
                to_hi(lo, c).wait_recv()

                @pl.when(has_hi)
                def _():
                    to_hi(lo, c).start()

            @pl.when(hi < nb)
            def _():
                add_chunk(acc_hi, hi, c)

            @pl.when(lo >= 0)
            def _():
                add_chunk(acc_lo, lo, c)

            return carry

        lax.fori_loop(0, chunks, chunk, 0)

        @pl.when(hi < nb)
        def _():
            finish(acc_hi, hi)

        @pl.when(lo >= 0)
        def _():
            finish(acc_lo, lo)

        return carry

    lax.fori_loop(1, nb, step, 0)

    def drain(b, carry):
        def drain_chunk(c, carry):
            @pl.when(has_lo & (b >= z))
            def _():
                to_lo(b, c).wait_send()

            @pl.when(has_hi & (b <= z))
            def _():
                to_hi(b, c).wait_send()

            return carry

        lax.fori_loop(0, chunks, drain_chunk, 0)
        own_copy(b).wait()
        for d in range(1, nd):
            part_copy(b, d).wait()
        return carry

    lax.fori_loop(0, nb, drain, 0)


def body(train_grads, query_grads, precond, candidates):
    rows, depth = train_grads.shape
    width = query_grads.shape[0]
    nb, nd = lax.axis_size("blk"), lax.axis_size("dim")
    chunks = 4
    half = rows // nd
    own, got = pl.pallas_call(
        functools.partial(kernel, nb, nd),
        out_shape=(
            jax.ShapeDtypeStruct((half, nb * width), jnp.float32),
            jax.ShapeDtypeStruct((nd - 1, half, nb * width), jnp.bfloat16),
        ),
        in_specs=[
            pl.BlockSpec(memory_space=pltpu.VMEM),
            pl.BlockSpec(memory_space=pltpu.VMEM),
            pl.BlockSpec(memory_space=pltpu.SMEM),
            pl.BlockSpec(memory_space=pl.ANY),
        ],
        out_specs=(pl.BlockSpec(memory_space=pl.ANY), pl.BlockSpec(memory_space=pl.ANY)),
        scratch_shapes=[
            pltpu.VMEM((chunks, rows, depth // chunks), jnp.bfloat16),
            pltpu.VMEM((nb, chunks, width, depth // chunks), jnp.bfloat16),
            pltpu.VMEM((rows, width), jnp.float32),
            pltpu.VMEM((rows, width), jnp.float32),
            pltpu.VMEM((nb, half, width), jnp.float32),
            pltpu.VMEM((nd - 1, nb, half, width), jnp.bfloat16),
            pltpu.SemaphoreType.DMA((chunks,)),
            pltpu.SemaphoreType.DMA((nb, chunks)),
            pltpu.SemaphoreType.DMA((nb, chunks)),
            pltpu.SemaphoreType.DMA((nb, chunks)),
            pltpu.SemaphoreType.DMA((nd - 1, nb)),
            pltpu.SemaphoreType.DMA((nd - 1, nb)),
            pltpu.SemaphoreType.DMA((nb,)),
        ],
        compiler_params=pltpu.CompilerParams(
            collective_id=0, has_side_effects=True, vmem_limit_bytes=44 * 2**20
        ),
    )(query_grads, precond[None, :], candidates, train_grads)
    total = own
    for d in range(nd - 1):
        total = total + got[d].astype(jnp.float32)
    return total


def solution(mesh):
    in_specs = (
        P(("groups", "blk"), "dim"),
        P(("groups", "rep", "blk"), "dim"),
        P("dim"),
        P(("groups", "blk"), "rep"),
    )
    out_specs = P(("groups", "blk", "dim"), "rep")
    return jax.shard_map(body, mesh=mesh, in_specs=in_specs, out_specs=out_specs, check_vma=False)
```

time: 156 us -> 83.4 us (0.53)
  waiting for transfers between devices: 107 us -> 0 us
  Pallas kernels: 0 us -> 79.3 us
  matrix products: 23.5 us -> 0 us
  between operations: 13.5 us -> 0.01 us
  starting transfers between devices: 3.2 us -> 0 us
  local copies, waits for them, and re-layouts: 5.53 us -> 2.7 us
  other arithmetic: 3.23 us -> 1.13 us
    pallas_call x0 -> x1, Pallas kernels: none -> 79.3 us  [body(): pl.pallas_call(functools.partial(kernel, nb, nd), out_shape=(jax.ShapeDty...]
    ppermute x3 -> x0, waiting for transfers between devices: 77.1 us -> none  [from_behind(): lax.ppermute(array, axis, [(i, (i + by) % devices) for i in range(devices)])]
    reduce_scatter x1 -> x0, waiting for transfers between devices: 29.7 us -> none  [body(): lax.psum_scatter(masked.reshape(rows, width * blocks), 'dim', scatter_dim...]
    dot_general x4 -> x0, matrix products: 23.5 us -> none  [block_scores(): lax.dot_general(train_grads, piece, (((1,), (1,)), ((), ())), preferred_e...]
    ppermute x3 -> x0, starting transfers between devices: 3.19 us -> none  [from_behind(): lax.ppermute(array, axis, [(i, (i + by) % devices) for i in range(devices)])]
    while x3 -> x0, local copies, waits for them, and re-layouts: 2.91 us -> none
    mul x1 -> x0, other arithmetic: 1.81 us -> none  [body(): partial_value.reshape(tiles, rows // tiles, blocks, width)]
    unnamed x4 -> x5, local copies, waits for them, and re-layouts: 0.97 us -> 2.7 us
  transfers between devices with their start and end apart: 4 -> 0, of which waited for: 4 -> 0; matrix products, arithmetic and copies ran while one was open for 0% -> 0% of each run, Pallas kernels for 0% -> 0%
where the time goes in v1:
time: 83.4 us; the launch traced here: 83.1 us
  Pallas kernels  79.3 us (95%)
  local copies, waits for them, and re-layouts  2.7 us (3%)
  other arithmetic  1.13 us (1%)
    pallas_call x1, Pallas kernels, body(): pl.pallas_call(functools.partial(kernel, nb, nd), out_shape=(jax.ShapeDty...  79.3 us
    unnamed x5, local copies, waits for them, and re-layouts  2.7 us

profile of v1, /device:TPU:0, one launch (start us, length us, event | category | flops | bytes accessed | tf_op | source)
XLA Modules:
  0.0 83.1 jit_solution(12516124190554208864)
XLA Ops:
  0.0 0.8 copy.5.keep
  0.8 0.0 copy-start
  0.8 1.2 %copy-done = bf16[128,4096]{1,0:T(8,128)(2,1)S(1)} copy-done((bf16[128,4096]{1,0:T(8,128)(2,1)S(1)}, bf16[128,4096]{1,0:T(8,128)(2,1)}, u32[]{:S(2)}) %copy-start) | copy-done | bytes 1048600
  2.0 0.0 copy-start.1
  2.0 0.7 copy-done.1
  2.7 79.3 %shard_map.46 = (f32[512,512]{1,0:T(8,128)S(1)}, bf16[1,512,512]{2,1,0:T(8,128)(2,1)S(1)}) custom-call(bf16[128,4096]{1,0:T(8,128)(2,1)S(1)} %copy-done, f32[1,4096]{1,0:T(1,128)S(1)} %bitcast.4, s32[8,4]{1,0:T(8,128)S(1)} %copy.5.keep, bf16[1024,4096]{1,0:T(8,128)(2,1)} %train_hbm.1), custom_call_target="tpu_custom_call" | custom-call | tf_op jit(solution)/shard_map/pallas_call | solution.py:227
  82.0 1.1 %convert_add_fusion = f32[512,512]{1,0:T(8,128)} fusion(f32[512,512]{1,0:T(8,128)S(1)} %get-tuple-element.7, bf16[1,512,512]{2,1,0:T(8,128)(2,1)S(1)} %get-tuple-element.8), kind=kLoop, calls=%fused_computation | loop fusion | flops 524288 | bytes 2621440 | tf_op jit(solution)/shard_map/add | solution.py:261
Async XLA Ops:
  0.8 1.2 %copy-start = (bf16[128,4096]{1,0:T(8,128)(2,1)S(1)}, bf16[128,4096]{1,0:T(8,128)(2,1)}, u32[]{:S(2)}) copy-start(bf16[128,4096]{1,0:T(8,128)(2,1)} %query.1) | copy-start | bytes 3145732
  2.0 0.7 copy-start.1

commit v2 on v1

--- a/solution.py
+++ b/solution.py
@@ -11,19 +11,30 @@
 
 
 def kernel(
-    nb, nd, query, precond, keep, train_hbm, own_hbm, got_hbm,
-    train, held, acc_hi, acc_lo, out_buf, part_buf,
+    nb, nd, nr, query, precond, keep, train_hbm, own_hbm, got_hbm,
+    train, held, acc_hi, acc_lo, acc_off, out_buf, part_buf,
+    end_train, end_own, end_part, end_got, end_sum, back,
     train_sem, send_lo, send_hi, recv, part_send, part_recv, own_sem,
+    slice_send, slice_recv, twin_send, end_send, end_recv, back_send, back_recv,
 ):
     chunks, rows, depth = train.shape
+    lent = end_train.shape[0]
     width = held.shape[2]
     half = rows // nd
+    share = rows // nr
     tiles = keep.shape[0]
     tile = rows // tiles
     z = lax.axis_index("blk")
     x = lax.axis_index("dim")
+    r = lax.axis_index("rep")
     has_lo = z > 0
     has_hi = z < nb - 1
+    between = has_lo & has_hi
+    is_end = jnp.logical_not(between)
+    lo_host, hi_host = z == 1, z == nb - 2
+    is_host = lo_host | hi_host
+    outer = jnp.where(lo_host, 0, nb - 1)
+    host = jnp.where(has_lo, nb - 2, 1)
     barrier = pltpu.get_barrier_semaphore()
 
     @pl.when(has_lo)
@@ -38,6 +49,10 @@
         pl.semaphore_signal(
             barrier, inc=1, device_id={"dim": lax.rem(x + d, nd)}, device_id_type=MESH
         )
+    for d in range(1, nr):
+        pl.semaphore_signal(
+            barrier, inc=1, device_id={"rep": lax.rem(r + d, nr)}, device_id_type=MESH
+        )
 
     def load(c):
         return pltpu.make_async_copy(
@@ -59,6 +74,30 @@
             src_ref=held.at[b, c], dst_ref=held.at[b, c],
             send_sem=send_hi.at[b, c], recv_sem=recv.at[b, c],
             device_id={"blk": z + 1}, device_id_type=MESH,
+        )
+
+    def goes_lo(c):
+        return has_lo & ((z > 1) | (c >= lent))
+
+    def goes_hi(c):
+        return has_hi & ((z < nb - 2) | (c >= lent))
+
+    def share_of(owner):
+        return pl.ds(pl.multiple_of(owner * share, share), share)
+
+    def slice_copy(c):
+        return pltpu.make_async_remote_copy(
+            src_ref=train.at[c, share_of(r), :], dst_ref=end_train.at[c, share_of(r), :],
+            send_sem=slice_send.at[c], recv_sem=slice_recv.at[c, r],
+            device_id={"blk": host}, device_id_type=MESH,
+        )
+
+    def twin_copy(c, d, owner):
+        return pltpu.make_async_remote_copy(
+            src_ref=end_train.at[c, share_of(owner), :],
+            dst_ref=end_train.at[c, share_of(owner), :],
+            send_sem=twin_send.at[c, d - 1], recv_sem=slice_recv.at[c, owner],
+            device_id={"rep": lax.rem(r + d, nr)}, device_id_type=MESH,
         )
 
     def prepare(c):
@@ -67,43 +106,49 @@
         held[z, c] = (query[:, span].astype(jnp.float32) * scale).astype(jnp.bfloat16)
 
     prepare(0)
-    between = has_lo & has_hi
 
     @pl.when(between)
     def _():
-        pl.semaphore_wait(barrier, nd + 1)
-
-    @pl.when(jnp.logical_not(between))
-    def _():
-        pl.semaphore_wait(barrier, nd)
+        pl.semaphore_wait(barrier, nd + nr)
+
+    @pl.when(is_end)
+    def _():
+        pl.semaphore_wait(barrier, nd + nr - 1)
 
     for c in range(chunks):
         if c:
             prepare(c)
-
-        @pl.when(has_lo)
+        if c == lent:
+
+            @pl.when(is_end)
+            def _():
+                for e in range(lent):
+                    load(e).wait()
+                    slice_copy(e).start()
+
+        @pl.when(goes_lo(c))
         def _():
             to_lo(z, c).start()
 
-        @pl.when(has_hi)
+        @pl.when(goes_hi(c))
         def _():
             to_hi(z, c).start()
 
-    def add_chunk(acc, b, c):
+    def add_chunk(acc, source, b, c, first):
         block = held[b, c]
 
         def one(i, carry):
             at = pl.ds(pl.multiple_of(i * 256, 256), 256)
             value = lax.dot_general(
-                train[c, at, :], block, (((1,), (1,)), ((), ())),
+                source[c, at, :], block, (((1,), (1,)), ((), ())),
                 preferred_element_type=jnp.float32,
             )
 
-            @pl.when(c == 0)
+            @pl.when(c == first)
             def _():
                 acc[at, :] = value
 
-            @pl.when(c > 0)
+            @pl.when(c != first)
             def _():
                 acc[at, :] += value
 
@@ -125,6 +170,23 @@
             own_hbm.at[:, pl.ds(pl.multiple_of(b * width, width), width)],
             own_sem.at[b],
         )
+
+    def end_copy(b, d):
+        return pltpu.make_async_remote_copy(
+            src_ref=end_part.at[d - 1, b], dst_ref=end_got.at[d - 1, b],
+            send_sem=end_send.at[d - 1, b], recv_sem=end_recv.at[d - 1, b],
+            device_id={"dim": lax.rem(x + d, nd)}, device_id_type=MESH,
+        )
+
+    def back_copy(b, to):
+        return pltpu.make_async_remote_copy(
+            src_ref=end_sum.at[b], dst_ref=back.at[b],
+            send_sem=back_send.at[b], recv_sem=back_recv.at[b],
+            device_id={"blk": to}, device_id_type=MESH,
+        )
+
+    def tile_keep(i, b):
+        return keep[x * (half // tile) + i, b].astype(jnp.float32)
 
     def masked(acc, b, first):
         values = []
@@ -141,69 +203,154 @@
             part_copy(b, d).start()
         for i, value in enumerate(masked(acc, b, x)):
             out_buf[b, i * tile : (i + 1) * tile, :] = value
-        own_copy(b).start()
-
-    for c in range(chunks):
+
+        @pl.when(between | (b == z))
+        def _():
+            own_copy(b).start()
+
+    @pl.when(between)
+    def _():
+        for c in range(lent):
+            load(c).wait()
+
+    for c in range(lent, chunks):
         load(c).wait()
 
     def own_chunk(c, carry):
-        add_chunk(acc_hi, z, c)
+        add_chunk(acc_hi, train, z, c, 0)
         return carry
 
     lax.fori_loop(0, chunks, own_chunk, 0)
     finish(acc_hi, z)
 
+    def half_of(owner):
+        return pl.ds(pl.multiple_of(owner * half, half), half)
+
+    def help_end():
+        for c in range(lent):
+            slice_copy(c).wait_recv()
+            for d in range(1, nr):
+                twin_copy(c, d, r).start()
+        for c in range(lent):
+            for d in range(1, nr):
+                twin_copy(c, d, lax.rem(r + d, nr)).wait_recv()
+
+        def one_block(b, carry):
+            @pl.when(b != outer)
+            def _():
+                def one_chunk(c, carry):
+                    add_chunk(acc_off, end_train, b, c, 0)
+                    return carry
+
+                lax.fori_loop(0, lent, one_chunk, 0)
+                for d in range(1, nd):
+                    end_part[d - 1, b] = acc_off[half_of(lax.rem(x + d, nd)), :].astype(jnp.bfloat16)
+                    end_copy(b, d).start()
+                end_own[b] = acc_off[half_of(x), :]
+
+            return carry
+
+        lax.fori_loop(0, nb, one_block, 0)
+
+    first_far = jnp.where(is_end, lent, 0)
+
     def step(s, carry):
-        hi, lo = z + s, z - s
+        hi = jnp.where(hi_host & (s == 2), nb - 1, z + s)
+        lo = jnp.where(lo_host & (s == 2), 0, z - s)
+        has_a = hi < nb
+        has_b = lo >= 0
 
         def chunk(c, carry):
-            @pl.when(hi < nb)
+            early = c < lent
+            turn = (early & (s == 1)) | (jnp.logical_not(early) & (s == 2))
+            take_hi = has_a & (has_lo | jnp.logical_not(early)) & (jnp.logical_not(hi_host) | turn)
+            take_lo = has_b & (has_hi | jnp.logical_not(early)) & (jnp.logical_not(lo_host) | turn)
+
+            @pl.when(is_host & (s == nb - 2) & (c == lent))
+            def _():
+                help_end()
+
+            @pl.when(take_hi)
             def _():
                 to_lo(hi, c).wait_recv()
 
-                @pl.when(has_lo)
+                @pl.when(goes_lo(c))
                 def _():
                     to_lo(hi, c).start()
 
-            @pl.when(lo >= 0)
+            @pl.when(take_lo)
             def _():
                 to_hi(lo, c).wait_recv()
 
-                @pl.when(has_hi)
+                @pl.when(goes_hi(c))
                 def _():
                     to_hi(lo, c).start()
 
-            @pl.when(hi < nb)
-            def _():
-                add_chunk(acc_hi, hi, c)
-
-            @pl.when(lo >= 0)
-            def _():
-                add_chunk(acc_lo, lo, c)
+            @pl.when(take_hi)
+            def _():
+                add_chunk(acc_hi, train, hi, c, first_far)
+
+            @pl.when(take_lo)
+            def _():
+                add_chunk(acc_lo, train, lo, c, first_far)
 
             return carry
 
         lax.fori_loop(0, chunks, chunk, 0)
 
-        @pl.when(hi < nb)
+        @pl.when(has_a & (jnp.logical_not(hi_host) | (s == 2)))
         def _():
             finish(acc_hi, hi)
 
-        @pl.when(lo >= 0)
+        @pl.when(has_b & (jnp.logical_not(lo_host) | (s == 2)))
         def _():
             finish(acc_lo, lo)
 
         return carry
 
     lax.fori_loop(1, nb, step, 0)
+
+    @pl.when(is_host)
+    def _():
+        def one_block(b, carry):
+            @pl.when(b != outer)
+            def _():
+                for d in range(1, nd):
+                    end_copy(b, d).wait_recv()
+                value = end_own[b]
+                for d in range(1, nd):
+                    value += end_got[d - 1, b].astype(jnp.float32)
+                end_sum[b] = value.astype(jnp.bfloat16)
+                back_copy(b, outer).start()
+
+            return carry
+
+        lax.fori_loop(0, nb, one_block, 0)
+
+    @pl.when(is_end)
+    def _():
+        def one_block(k, carry):
+            b = jnp.where(has_lo, k, nb - 1 - k)
+
+            @pl.when(b != z)
+            def _():
+                back_copy(b, host).wait_recv()
+                for i in range(half // tile):
+                    at = slice(i * tile, (i + 1) * tile)
+                    out_buf[b, at, :] += back[b, at, :].astype(jnp.float32) * tile_keep(i, b)
+                own_copy(b).start()
+
+            return carry
+
+        lax.fori_loop(0, nb, one_block, 0)
 
     def drain(b, carry):
         def drain_chunk(c, carry):
-            @pl.when(has_lo & (b >= z))
+            @pl.when(goes_lo(c) & (b >= z))
             def _():
                 to_lo(b, c).wait_send()
 
-            @pl.when(has_hi & (b <= z))
+            @pl.when(goes_hi(c) & (b <= z))
             def _():
                 to_hi(b, c).wait_send()
 
@@ -213,19 +360,37 @@
         own_copy(b).wait()
         for d in range(1, nd):
             part_copy(b, d).wait()
+
+        @pl.when(is_host & (b != outer))
+        def _():
+            for d in range(1, nd):
+                end_copy(b, d).wait_send()
+            back_copy(b, outer).wait_send()
+
         return carry
 
     lax.fori_loop(0, nb, drain, 0)
+
+    @pl.when(is_end)
+    def _():
+        for c in range(lent):
+            slice_copy(c).wait_send()
+
+    @pl.when(is_host)
+    def _():
+        for c in range(lent):
+            for d in range(1, nr):
+                twin_copy(c, d, r).wait_send()
 
 
 def body(train_grads, query_grads, precond, candidates):
     rows, depth = train_grads.shape
     width = query_grads.shape[0]
-    nb, nd = lax.axis_size("blk"), lax.axis_size("dim")
-    chunks = 4
+    nb, nd, nr = (lax.axis_size(name) for name in ("blk", "dim", "rep"))
+    chunks, lent = 8, 2
     half = rows // nd
     own, got = pl.pallas_call(
-        functools.partial(kernel, nb, nd),
+        functools.partial(kernel, nb, nd, nr),
         out_shape=(
             jax.ShapeDtypeStruct((half, nb * width), jnp.float32),
             jax.ShapeDtypeStruct((nd - 1, half, nb * width), jnp.bfloat16),
@@ -242,14 +407,28 @@
             pltpu.VMEM((nb, chunks, width, depth // chunks), jnp.bfloat16),
             pltpu.VMEM((rows, width), jnp.float32),
             pltpu.VMEM((rows, width), jnp.float32),
+            pltpu.VMEM((rows, width), jnp.float32),
             pltpu.VMEM((nb, half, width), jnp.float32),
             pltpu.VMEM((nd - 1, nb, half, width), jnp.bfloat16),
+            pltpu.VMEM((lent, rows, depth // chunks), jnp.bfloat16),
+            pltpu.VMEM((nb, half, width), jnp.float32),
+            pltpu.VMEM((nd - 1, nb, half, width), jnp.bfloat16),
+            pltpu.VMEM((nd - 1, nb, half, width), jnp.bfloat16),
+            pltpu.VMEM((nb, half, width), jnp.bfloat16),
+            pltpu.VMEM((nb, half, width), jnp.bfloat16),
             pltpu.SemaphoreType.DMA((chunks,)),
             pltpu.SemaphoreType.DMA((nb, chunks)),
             pltpu.SemaphoreType.DMA((nb, chunks)),
             pltpu.SemaphoreType.DMA((nb, chunks)),
             pltpu.SemaphoreType.DMA((nd - 1, nb)),
             pltpu.SemaphoreType.DMA((nd - 1, nb)),
+            pltpu.SemaphoreType.DMA((nb,)),
+            pltpu.SemaphoreType.DMA((lent,)),
+            pltpu.SemaphoreType.DMA((lent, nr)),
+            pltpu.SemaphoreType.DMA((lent, nr)),
+            pltpu.SemaphoreType.DMA((nd - 1, nb)),
+            pltpu.SemaphoreType.DMA((nd - 1, nb)),
+            pltpu.SemaphoreType.DMA((nb,)),
             pltpu.SemaphoreType.DMA((nb,)),
         ],
         compiler_params=pltpu.CompilerParams(

time: 83.4 us -> 114 us (1.37)
  Pallas kernels: 79.3 us -> 110 us
    pallas_call x1, Pallas kernels: 79.3 us -> 110 us  [body(): pl.pallas_call(functools.partial(kernel, nb, nd, nr), out_shape=(jax.Shap...]
where the time goes in v2:
time: 114 us
  Pallas kernels  110 us (96%)
  local copies, waits for them, and re-layouts  2.7 us (2%)
    pallas_call x1, Pallas kernels, body(): pl.pallas_call(functools.partial(kernel, nb, nd, nr), out_shape=(jax.Shap...  110 us
    unnamed x5, local copies, waits for them, and re-layouts  2.7 us

profile of v2, /device:TPU:0, one launch (start us, length us, event | category | flops | bytes accessed | tf_op | source)
XLA Modules:
  0.0 113.5 jit_solution(12501761220233166027)
XLA Ops:
  0.0 0.8 copy.5.keep
  0.8 0.0 copy-start
  0.8 1.2 %copy-done = bf16[128,4096]{1,0:T(8,128)(2,1)S(1)} copy-done((bf16[128,4096]{1,0:T(8,128)(2,1)S(1)}, bf16[128,4096]{1,0:T(8,128)(2,1)}, u32[]{:S(2)}) %copy-start) | copy-done | bytes 1048600
  2.0 0.0 copy-start.1
  2.0 0.7 copy-done.1
  2.7 109.7 %shard_map.46 = (f32[512,512]{1,0:T(8,128)S(1)}, bf16[1,512,512]{2,1,0:T(8,128)(2,1)S(1)}) custom-call(bf16[128,4096]{1,0:T(8,128)(2,1)S(1)} %copy-done, f32[1,4096]{1,0:T(1,128)S(1)} %bitcast.4, s32[8,4]{1,0:T(8,128)S(1)} %copy.5.keep, bf16[1024,4096]{1,0:T(8,128)(2,1)} %train_hbm.1), custom_call_target="tpu_custom_call" | custom-call | tf_op jit(solution)/shard_map/pallas_call | solution.py:392
  112.4 1.1 convert_add_fusion
Async XLA Ops:
  0.8 1.2 %copy-start = (bf16[128,4096]{1,0:T(8,128)(2,1)S(1)}, bf16[128,4096]{1,0:T(8,128)(2,1)}, u32[]{:S(2)}) copy-start(bf16[128,4096]{1,0:T(8,128)(2,1)} %query.1) | copy-start | bytes 3145732
  2.0 0.7 copy-start.1

commit v3 on v2

--- a/solution.py
+++ b/solution.py
@@ -11,7 +11,7 @@
 
 
 def kernel(
-    nb, nd, nr, query, precond, keep, train_hbm, own_hbm, got_hbm,
+    nb, nd, nr, lag, query, precond, keep, train_hbm, own_hbm, got_hbm,
     train, held, acc_hi, acc_lo, acc_off, out_buf, part_buf,
     end_train, end_own, end_part, end_got, end_sum, back,
     train_sem, send_lo, send_hi, recv, part_send, part_recv, own_sem,
@@ -137,24 +137,17 @@
     def add_chunk(acc, source, b, c, first):
         block = held[b, c]
 
-        def one(i, carry):
-            at = pl.ds(pl.multiple_of(i * 256, 256), 256)
-            value = lax.dot_general(
-                source[c, at, :], block, (((1,), (1,)), ((), ())),
-                preferred_element_type=jnp.float32,
-            )
-
-            @pl.when(c == first)
-            def _():
-                acc[at, :] = value
-
-            @pl.when(c != first)
-            def _():
-                acc[at, :] += value
-
-            return carry
-
-        lax.fori_loop(0, rows // 256, one, 0)
+        value = lax.dot_general(
+            source[c], block, (((1,), (1,)), ((), ())), preferred_element_type=jnp.float32
+        )
+
+        @pl.when(c == first)
+        def _():
+            acc[...] = value
+
+        @pl.when(c != first)
+        def _():
+            acc[...] += value
 
     def part_copy(b, d):
         return pltpu.make_async_remote_copy(
@@ -260,43 +253,54 @@
         has_a = hi < nb
         has_b = lo >= 0
 
-        def chunk(c, carry):
-            early = c < lent
-            turn = (early & (s == 1)) | (jnp.logical_not(early) & (s == 2))
-            take_hi = has_a & (has_lo | jnp.logical_not(early)) & (jnp.logical_not(hi_host) | turn)
-            take_lo = has_b & (has_hi | jnp.logical_not(early)) & (jnp.logical_not(lo_host) | turn)
-
-            @pl.when(is_host & (s == nb - 2) & (c == lent))
+        second = is_host & (s == 2)
+
+        def chunk(i, carry):
+            late = second & (i >= lent)
+            inner_c = jnp.where(late, i - lag, i)
+            inner_ok = (inner_c < chunks) & (jnp.logical_not(late) | (i >= lent + lag))
+            outer_c = jnp.where(s == 1, i - (chunks - lent), i)
+            outer_ok = (outer_c < chunks) & (
+                ((s == 1) & (outer_c >= 0) & (outer_c < lent)) | ((s == 2) & (outer_c >= lent))
+            )
+            hi_c = jnp.where(hi_host, outer_c, inner_c)
+            lo_c = jnp.where(lo_host, outer_c, inner_c)
+            hi_ok = (hi_host & outer_ok) | (jnp.logical_not(hi_host) & inner_ok)
+            lo_ok = (lo_host & outer_ok) | (jnp.logical_not(lo_host) & inner_ok)
+            take_hi = has_a & hi_ok & (has_lo | (hi_c >= lent))
+            take_lo = has_b & lo_ok & (has_hi | (lo_c >= lent))
+
+            @pl.when(is_host & (s == nb - 2) & (i == lent))
             def _():
                 help_end()
 
             @pl.when(take_hi)
             def _():
-                to_lo(hi, c).wait_recv()
-
-                @pl.when(goes_lo(c))
+                to_lo(hi, hi_c).wait_recv()
+
+                @pl.when(goes_lo(hi_c))
                 def _():
-                    to_lo(hi, c).start()
+                    to_lo(hi, hi_c).start()
 
             @pl.when(take_lo)
             def _():
-                to_hi(lo, c).wait_recv()
-
-                @pl.when(goes_hi(c))
+                to_hi(lo, lo_c).wait_recv()
+
+                @pl.when(goes_hi(lo_c))
                 def _():
-                    to_hi(lo, c).start()
+                    to_hi(lo, lo_c).start()
 
             @pl.when(take_hi)
             def _():
-                add_chunk(acc_hi, train, hi, c, first_far)
+                add_chunk(acc_hi, train, hi, hi_c, first_far)
 
             @pl.when(take_lo)
             def _():
-                add_chunk(acc_lo, train, lo, c, first_far)
+                add_chunk(acc_lo, train, lo, lo_c, first_far)
 
             return carry
 
-        lax.fori_loop(0, chunks, chunk, 0)
+        lax.fori_loop(0, chunks + lag, chunk, 0)
 
         @pl.when(has_a & (jnp.logical_not(hi_host) | (s == 2)))
         def _():
@@ -387,10 +391,10 @@
     rows, depth = train_grads.shape
     width = query_grads.shape[0]
     nb, nd, nr = (lax.axis_size(name) for name in ("blk", "dim", "rep"))
-    chunks, lent = 8, 2
+    chunks, lent, lag = 8, 2, 2
     half = rows // nd
     own, got = pl.pallas_call(
-        functools.partial(kernel, nb, nd, nr),
+        functools.partial(kernel, nb, nd, nr, lag),
         out_shape=(
             jax.ShapeDtypeStruct((half, nb * width), jnp.float32),
             jax.ShapeDtypeStruct((nd - 1, half, nb * width), jnp.bfloat16),

time: 114 us -> 77.8 us (0.68)
  Pallas kernels: 110 us -> 73.7 us
    pallas_call x1, Pallas kernels: 110 us -> 73.7 us  [body(): pl.pallas_call(functools.partial(kernel, nb, nd, nr, lag), out_shape=(jax...]
where the time goes in v3:
time: 77.8 us; the launch traced here: 77.5 us
  Pallas kernels  73.7 us (95%)
  local copies, waits for them, and re-layouts  2.7 us (3%)
  other arithmetic  1.13 us (1%)
    pallas_call x1, Pallas kernels, body(): pl.pallas_call(functools.partial(kernel, nb, nd, nr, lag), out_shape=(jax...  73.7 us
    unnamed x5, local copies, waits for them, and re-layouts  2.7 us

profile of v3, /device:TPU:0, one launch (start us, length us, event | category | flops | bytes accessed | tf_op | source)
XLA Modules:
  0.0 77.5 jit_solution(6135027216251049483)
XLA Ops:
  0.0 0.8 copy.5.keep
  0.8 0.0 copy-start
  0.8 1.2 %copy-done = bf16[128,4096]{1,0:T(8,128)(2,1)S(1)} copy-done((bf16[128,4096]{1,0:T(8,128)(2,1)S(1)}, bf16[128,4096]{1,0:T(8,128)(2,1)}, u32[]{:S(2)}) %copy-start) | copy-done | bytes 1048600
  2.0 0.0 copy-start.1
  2.0 0.7 copy-done.1
  2.7 73.7 %shard_map.46 = (f32[512,512]{1,0:T(8,128)S(1)}, bf16[1,512,512]{2,1,0:T(8,128)(2,1)S(1)}) custom-call(bf16[128,4096]{1,0:T(8,128)(2,1)S(1)} %copy-done, f32[1,4096]{1,0:T(1,128)S(1)} %bitcast.4, s32[8,4]{1,0:T(8,128)S(1)} %copy.5.keep, bf16[1024,4096]{1,0:T(8,128)(2,1)} %train_hbm.1), custom_call_target="tpu_custom_call" | custom-call | tf_op jit(solution)/shard_map/pallas_call | solution.py:396
  76.4 1.1 %convert_add_fusion = f32[512,512]{1,0:T(8,128)} fusion(f32[512,512]{1,0:T(8,128)S(1)} %get-tuple-element.7, bf16[1,512,512]{2,1,0:T(8,128)(2,1)S(1)} %get-tuple-element.8), kind=kLoop, calls=%fused_computation | loop fusion | flops 524288 | bytes 2621440 | tf_op jit(solution)/shard_map/add | solution.py:444
Async XLA Ops:
  0.8 1.2 %copy-start = (bf16[128,4096]{1,0:T(8,128)(2,1)S(1)}, bf16[128,4096]{1,0:T(8,128)(2,1)}, u32[]{:S(2)}) copy-start(bf16[128,4096]{1,0:T(8,128)(2,1)} %query.1) | copy-start | bytes 3145732
  2.0 0.7 copy-start.1

commit v4 on v3

--- a/solution.py
+++ b/solution.py
@@ -118,7 +118,7 @@
     for c in range(chunks):
         if c:
             prepare(c)
-        if c == lent:
+        if c == 1:
 
             @pl.when(is_end)
             def _():

time: 77.8 us -> 80.1 us (1.030)
  Pallas kernels: 73.7 us -> 75.3 us
    pallas_call x1, Pallas kernels: 73.7 us -> 75.3 us  [body(): pl.pallas_call(functools.partial(kernel, nb, nd, nr, lag), out_shape=(jax...]
where the time goes in v4:
time: 80.1 us; the launch traced here: 79.1 us
  Pallas kernels  75.3 us (94%)
  local copies, waits for them, and re-layouts  2.7 us (3%)
  other arithmetic  1.13 us (1%)
    pallas_call x1, Pallas kernels, body(): pl.pallas_call(functools.partial(kernel, nb, nd, nr, lag), out_shape=(jax...  75.3 us
    unnamed x5, local copies, waits for them, and re-layouts  2.7 us

profile of v4, /device:TPU:0, one launch (start us, length us, event | category | flops | bytes accessed | tf_op | source)
XLA Modules:
  0.0 79.1 jit_solution(8301815917825058674)
XLA Ops:
  0.0 0.8 copy.5.keep
  0.8 0.0 copy-start
  0.8 1.2 %copy-done = bf16[128,4096]{1,0:T(8,128)(2,1)S(1)} copy-done((bf16[128,4096]{1,0:T(8,128)(2,1)S(1)}, bf16[128,4096]{1,0:T(8,128)(2,1)}, u32[]{:S(2)}) %copy-start) | copy-done | bytes 1048600
  2.0 0.0 copy-start.1
  2.0 0.7 copy-done.1
  2.7 75.3 %shard_map.46 = (f32[512,512]{1,0:T(8,128)S(1)}, bf16[1,512,512]{2,1,0:T(8,128)(2,1)S(1)}) custom-call(bf16[128,4096]{1,0:T(8,128)(2,1)S(1)} %copy-done, f32[1,4096]{1,0:T(1,128)S(1)} %bitcast.4, s32[8,4]{1,0:T(8,128)S(1)} %copy.5.keep, bf16[1024,4096]{1,0:T(8,128)(2,1)} %train_hbm.1), custom_call_target="tpu_custom_call" | custom-call | tf_op jit(solution)/shard_map/pallas_call | solution.py:396
  78.0 1.1 %convert_add_fusion = f32[512,512]{1,0:T(8,128)} fusion(f32[512,512]{1,0:T(8,128)S(1)} %get-tuple-element.7, bf16[1,512,512]{2,1,0:T(8,128)(2,1)S(1)} %get-tuple-element.8), kind=kLoop, calls=%fused_computation | loop fusion | flops 524288 | bytes 2621440 | tf_op jit(solution)/shard_map/add | solution.py:444
Async XLA Ops:
  0.8 1.2 %copy-start = (bf16[128,4096]{1,0:T(8,128)(2,1)S(1)}, bf16[128,4096]{1,0:T(8,128)(2,1)}, u32[]{:S(2)}) copy-start(bf16[128,4096]{1,0:T(8,128)(2,1)} %query.1) | copy-start | bytes 3145732
  2.0 0.7 copy-start.1
